TPU v7x, 32 devices: a whole 2x2x4 slice. The times are simulated.
32 devices in a mesh: grp: 2 (over y), gx: 4 (over z), trc: 2 (over x), gy: 2 (over core).
Axes of the slice: x: 2, y: 2, z: 4, core: 2. Of those that a mesh axis runs over, the one named last changes fastest.
Arguments:
- tracers: float32 [16, 8, 180, 256], P(('grp', 'trc'), None, 'gx', 'gy'), parts along dimension 0, may hold values from -6 to 6
- colors: int32 [8, 180, 256], P(None, 'gx', 'gy'), may hold values from 0 to 7
- land_mask: int32 [8, 180, 256], P('trc', 'gx', 'gy'), may hold values 0 or 1
- east_velocity: float32 [8, 180, 256], P('trc', 'gx', 'gy'), may hold values from -2 to 2
- north_velocity: float32 [8, 180, 256], P('trc', 'gx', 'gy'), may hold values from -2 to 2
- mixing: float32 [8, 180, 256], P('trc', 'gx', 'gy'), may hold values from 0.01 to 0.1
- slope_east: float32 [8, 180, 256], P('trc', 'gx', 'gy'), may hold values from -2.5 to 2.5
- slope_north: float32 [8, 180, 256], P('trc', 'gx', 'gy'), may hold values from -2.5 to 2.5
Outputs:
- advanced: float32 [16, 8, 180, 256], P(('grp', 'trc'), None, 'gx', 'gy'), parts along dimension 0
There are 2 independent parts, one for each index of `grp`. A program takes and returns all parts, laid end to end along the dimension named above; an argument that names none is the same for every part. Nothing has to cross between parts.
Inputs may be any that keep to these rules, and one draw needn't show every extreme that they name: colors name tracers of one batch.
All inputs are finite; a program needn't handle non-finite values. No bound on the sum of `land_mask` on one device may be relied on, other than what follows from the above.
Results may differ from a plain program's by a relative error of at most 0.0003.
Values sent between devices are 32-bit elements; how exact they have to be, the bound alone decides.
A program may use at most 64 MiB of HBM per device.

v0:
```python
import jax
import jax.numpy as jnp
from jax import lax
from jax.sharding import PartitionSpec as P

SUBSTEPS = 4


time_step = 0.8
pulse_height = 1.0


def from_partner(array, axis, bit):
    return lax.ppermute(array, axis, [(i, i ^ 1 << bit) for i in range(lax.axis_size(axis))])


def padded_2(block, sides, width, periodic):
    for axis, dim in sides:
        count = lax.axis_size(axis)
        forward = [(i, i + 1) for i in range(count - 1)]
        if periodic:
            forward.append((count - 1, 0))
        backward = [(target, source) for source, target in forward]
        low = lax.ppermute(
            lax.slice_in_dim(block, block.shape[dim] - width, None, axis=dim), axis, forward
        )
        high = lax.ppermute(lax.slice_in_dim(block, 0, width, axis=dim), axis, backward)
        block = jnp.concatenate([low, block, high], axis=dim)
    return block


def vertical(field):
    padded = jnp.pad(field, ((0, 0), (1, 1), (0, 0), (0, 0)))
    return 0.5 * (padded[:, 2:] - padded[:, :-2])


def mirror_fold(framed, margin, lat_rows, at_top, gx_count):
    edge_row = framed[:, :, :, margin + lat_rows - 1]
    for bit_index in range(gx_count.bit_length() - 1):
        edge_row = from_partner(edge_row, "gx", bit_index)
    mirror = edge_row[:, :, ::-1]
    above = margin + lat_rows
    top_row = jnp.where(at_top, mirror, framed[:, :, :, above])
    return framed.at[:, :, :, above].set(top_row)


def advance_window(framed, window, margin, lat_rows, at_top):
    width = framed.shape[2]
    height = framed.shape[3]
    slopes = vertical(framed)
    east_speed = window[0, :, 0 : width - 1, 1 : height - 1]
    mixing_east = window[2, :, 0 : width - 1, 1 : height - 1]
    slope_along = window[3, :, 0 : width - 1, 1 : height - 1]
    open_east = window[5, :, 0 : width - 1, 1 : height - 1] * window[5, :, 1:width, 1 : height - 1]
    north_speed = window[1, :, 1 : width - 1, 0 : height - 1]
    mixing_north = window[2, :, 1 : width - 1, 0 : height - 1]
    slope_across = window[4, :, 1 : width - 1, 0 : height - 1]
    wet_here = window[5, :, 1 : width - 1, 0 : height - 1]
    wet_above = window[5, :, 1 : width - 1, 1:height]
    row_index = jnp.arange(height - 1, dtype=jnp.int32)
    wet_above = jnp.where(
        at_top & (row_index == margin + lat_rows - 1), jnp.float32(1.0), wet_above
    )
    open_north = wet_here * wet_above
    wet_inner = window[5, :, 1 : width - 1, 1 : height - 1]
    here_x = framed[:, :, 0 : width - 1, 1 : height - 1]
    east_x = framed[:, :, 1:width, 1 : height - 1]
    slope_hx = slopes[:, :, 0 : width - 1, 1 : height - 1]
    slope_ex = slopes[:, :, 1:width, 1 : height - 1]
    flux_east = (
        jnp.maximum(east_speed, 0.0) * here_x
        + jnp.minimum(east_speed, 0.0) * east_x
        - mixing_east * (east_x - here_x)
        - mixing_east * slope_along * (0.5 * (slope_hx + slope_ex))
    ) * open_east
    here_y = framed[:, :, 1 : width - 1, 0 : height - 1]
    north_y = framed[:, :, 1 : width - 1, 1:height]
    slope_hy = slopes[:, :, 1 : width - 1, 0 : height - 1]
    slope_ny = slopes[:, :, 1 : width - 1, 1:height]
    flux_north = (
        jnp.maximum(north_speed, 0.0) * here_y
        + jnp.minimum(north_speed, 0.0) * north_y
        - mixing_north * (north_y - here_y)
        - mixing_north * slope_across * (0.5 * (slope_hy + slope_ny))
    ) * open_north
    inner = framed[:, :, 1 : width - 1, 1 : height - 1]
    return inner - time_step * (
        wet_inner
        * (
            flux_east[:, :, 1:]
            - flux_east[:, :, :-1]
            + (flux_north[:, :, :, 1:] - flux_north[:, :, :, :-1])
        )
    )


def local(
    tracers, colors, land_mask, east_velocity, north_velocity, mixing, slope_east, slope_north
):
    tracer_count, levels, columns, lat_rows = tracers.shape
    rim_width = 1
    stacked = jnp.stack(
        [
            east_velocity,
            north_velocity,
            mixing,
            slope_east,
            slope_north,
            land_mask.astype(jnp.float32),
        ]
    )
    whole_fields = lax.all_gather(stacked, "trc", axis=1, tiled=True)
    widened = padded_2(whole_fields, (("gx", 2),), rim_width, True)
    fields = padded_2(widened, (("gy", 3),), rim_width, False)
    wet_mask = fields[5, :, rim_width : rim_width + columns, rim_width : rim_width + lat_rows]
    first_label = lax.axis_index("trc") * tracer_count
    labels = first_label + jnp.arange(tracer_count, dtype=jnp.int32)
    pulses = jnp.where(
        colors[None] == labels[:, None, None, None], wet_mask[None], jnp.float32(0.0)
    )
    concentration = tracers + pulse_height * pulses
    at_top = lax.axis_index("gy") == lax.axis_size("gy") - 1
    gx_count = lax.axis_size("gx")
    for substep in range(SUBSTEPS):
        wide_conc = padded_2(concentration, (("gx", 2),), 1, True)
        framed_conc = padded_2(wide_conc, (("gy", 3),), 1, False)
        framed_conc = mirror_fold(framed_conc, 1, lat_rows, at_top, gx_count)
        concentration = advance_window(framed_conc, fields, 1, lat_rows, at_top)
    return concentration


def solution(mesh):
    in_specs = (
        P(("grp", "trc"), None, "gx", "gy"),
        P(None, "gx", "gy"),
        P("trc", "gx", "gy"),
        P("trc", "gx", "gy"),
        P("trc", "gx", "gy"),
        P("trc", "gx", "gy"),
        P("trc", "gx", "gy"),
        P("trc", "gx", "gy"),
    )
    out_specs = P(("grp", "trc"), None, "gx", "gy")
    return jax.shard_map(local, mesh=mesh, in_specs=in_specs, out_specs=out_specs, check_vma=False)
```

profile of v0, /device:TPU:0, one launch (start us, length us, event | category | flops | bytes accessed | tf_op | source)
XLA Modules:
  0.0 228.5 jit_solution(16917465116726724181)
XLA Ops:
  12.9 25.6 %all-gather.2.cloned.1.call-done = f32[6,8,45,128]{3,2,0,1:T(8,128)} async-done(((f32[6,4,45,128]{3,2,0,1:T(8,128)}), f32[6,8,45,128]{3,2,0,1:T(8,128)}) %all-gather.2.cloned.1.call-update) | async-done | bytes 1105936 | tf_op jit(solution)/shard_map/all_gather | solution.py:112
  41.2 2.3 %collective-permute-start.1 = (f32[4,8,1,128]{3,1,2,0:T(8,128)S(1)}, f32[4,8,1,128]{3,1,2,0:T(8,128)S(1)}, u32[]{:S(2)}, u32[]{:S(2)}) collective-permute-start(f32[4,8,1,128]{3,1,2,0:T(8,128)S(1)} %get-tuple-element.81), channel_id=1, source_target_pairs={{4,0},{8,4},{12,8},{0,12},{5,1},{9,5},{13,9},{1,13},{6,2},{10,6},{... | collective-permute-start | bytes 49160 | tf_op jit(solution)/shard_map/ppermute | solution.py:27
  48.3 3.0 %collective-permute-start.2 = (f32[4,8,47,1]{2,1,0,3:T(8,128)}, f32[4,8,47,1]{2,1,0,3:T(8,128)S(1)}, u32[]{:S(2)}, u32[]{:S(2)}) collective-permute-start(f32[4,8,47,1]{2,1,0,3:T(8,128)} %copy.123), channel_id=1, source_target_pairs={{0,1},{2,3},{4,5},{6,7},{8,9},{10,11},{12,13},{14,15},{16,17},{18,... | collective-permute-start | bytes 18056 | tf_op jit(solution)/shard_map/ppermute | solution.py:24
  54.1 2.9 %collective-permute-start.7 = (f32[6,8,1,128]{3,2,0,1:T(1,128)}, f32[6,8,1,128]{3,2,0,1:T(1,128)S(1)}, u32[]{:S(2)}, u32[]{:S(2)}) collective-permute-start(f32[6,8,1,128]{3,2,0,1:T(1,128)} %get-tuple-element.65), channel_id=1, source_target_pairs={{4,0},{8,4},{12,8},{0,12},{5,1},{9,5},{13,9},{1,13},{6,2},{10,6},{... | collective-permute-start | bytes 73736 | tf_op jit(solution)/shard_map/ppermute | solution.py:27
  60.9 2.0 pad_maximum_fusion
  67.4 2.3 %copy.99 = f32[6,8,47,1]{2,1,3,0:T(8,128)} copy(f32[6,8,47,1]{3,2,0,1:T(8,128)} %get-tuple-element.62) | data formatting | bytes 18048 | tf_op jit(solution)/shard_map/slice | solution.py:25
  72.1 4.2 %collective-permute-start.8 = (f32[6,8,47,1]{2,1,3,0:T(8,128)}, f32[6,8,47,1]{2,1,3,0:T(8,128)}, u32[]{:S(2)}, u32[]{:S(2)}) collective-permute-start(f32[6,8,47,1]{2,1,3,0:T(8,128)} %copy.99), channel_id=1, source_target_pairs={{0,1},{2,3},{4,5},{6,7},{8,9},{10,11},{12,13},{14,15},{16,17},{18,... | collective-permute-start | bytes 27080 | tf_op jit(solution)/shard_map/ppermute | solution.py:24
  77.5 15.1 %scatter.14 = f32[4,8,47,130]{3,1,2,0:T(8,128)S(1)} dynamic-update-slice(f32[4,8,47,130]{3,1,2,0:T(8,128)S(1)} %pad_maximum_fusion, f32[4,8,47,1]{3,1,2,0:T(8,128)S(1)} %copy.93, s32[]{:T(128)} %constant.109.clone.1, s32[]{:T(128)} %constant.109.clone.1, s32[]{:T(128)} %constant.109.clone.1, s32[]{:T(128)} %constant.110.clone.1) | dynamic-update-slice | bytes 12036 | tf_op jit(solution)/shard_map/scatter | solution.py:44
  95.5 2.3 %copy.100 = f32[6,8,47,1]{3,2,0,1:T(8,128)} copy(f32[6,8,47,1]{2,1,3,0:T(8,128)} %collective-permute-done.8) | data formatting | bytes 18048 | tf_op jit(solution)/shard_map/ppermute | solution.py:24
  97.8 2.3 %copy.106 = f32[6,8,47,1]{3,2,0,1:T(8,128)} copy(f32[6,8,47,1]{2,1,3,0:T(8,128)} %collective-permute-done.9) | data formatting | bytes 18048 | tf_op jit(solution)/shard_map/ppermute | solution.py:27
  106.8 2.5 %collective-permute-start.11 = (f32[4,8,1,128]{3,1,2,0:T(8,128)S(1)}, f32[4,8,1,128]{3,1,2,0:T(8,128)S(1)}, u32[]{:S(2)}, u32[]{:S(2)}) collective-permute-start(f32[4,8,1,128]{3,1,2,0:T(8,128)S(1)} %get-tuple-element.79), channel_id=1, source_target_pairs={{4,0},{8,4},{12,8},{0,12},{5,1},{9,5},{13,9},{1,13},{6,2},{10,6},{... | collective-permute-start | bytes 49160 | tf_op jit(solution)/shard_map/ppermute | solution.py:27
  115.4 3.7 %collective-permute-start.15 = (f32[4,8,47]{2,1,0:T(8,128)S(1)}, f32[4,8,47]{2,1,0:T(8,128)S(1)}, u32[]{:S(2)}, u32[]{:S(2)}) collective-permute-start(f32[4,8,47]{2,1,0:T(8,128)S(1)} %collective-permute-done.14), channel_id=1, source_target_pairs={{0,8},{4,12},{8,0},{12,4},{1,9},{5,13},{9,1},{13,5},{2,10},{6,14},... | collective-permute-start | bytes 18056 | tf_op jit(solution)/shard_map/ppermute | solution.py:14
  120.8 1.8 pad_maximum_fusion.1
  123.0 15.1 %scatter.15 = f32[4,8,47,130]{3,1,2,0:T(8,128)S(1)} dynamic-update-slice(f32[4,8,47,130]{3,1,2,0:T(8,128)S(1)} %pad_maximum_fusion.1, f32[4,8,47,1]{3,1,2,0:T(8,128)S(1)} %copy.112, s32[]{:T(128)} %constant.109.clone.1, s32[]{:T(128)} %constant.109.clone.1, s32[]{:T(128)} %constant.109.clone.1, s32[]{:T(128)} %constant.110.clone.1) | dynamic-update-slice | bytes 12036 | tf_op jit(solution)/shard_map/scatter | solution.py:44
  143.0 3.1 %collective-permute-start.17 = (f32[4,8,1,128]{3,1,2,0:T(8,128)S(1)}, f32[4,8,1,128]{3,1,2,0:T(8,128)S(1)}, u32[]{:S(2)}, u32[]{:S(2)}) collective-permute-start(f32[4,8,1,128]{3,1,2,0:T(8,128)S(1)} %get-tuple-element.77), channel_id=1, source_target_pairs={{4,0},{8,4},{12,8},{0,12},{5,1},{9,5},{13,9},{1,13},{6,2},{10,6},{... | collective-permute-start | bytes 49160 | tf_op jit(solution)/shard_map/ppermute | solution.py:27
  146.1 1.9 collective-permute-done.16
  152.5 3.7 %collective-permute-start.21 = (f32[4,8,47]{2,1,0:T(8,128)S(1)}, f32[4,8,47]{2,1,0:T(8,128)S(1)}, u32[]{:S(2)}, u32[]{:S(2)}) collective-permute-start(f32[4,8,47]{2,1,0:T(8,128)S(1)} %collective-permute-done.20), channel_id=1, source_target_pairs={{0,8},{4,12},{8,0},{12,4},{1,9},{5,13},{9,1},{13,5},{2,10},{6,14},... | collective-permute-start | bytes 18056 | tf_op jit(solution)/shard_map/ppermute | solution.py:14
  158.7 2.2 pad_maximum_fusion.2
  162.3 16.0 %scatter.16 = f32[4,8,47,130]{3,1,2,0:T(8,128)S(1)} dynamic-update-slice(f32[4,8,47,130]{3,1,2,0:T(8,128)S(1)} %pad_maximum_fusion.2, f32[4,8,47,1]{3,1,2,0:T(8,128)} %copy.117, s32[]{:T(128)} %constant.109.clone.1, s32[]{:T(128)} %constant.109.clone.1, s32[]{:T(128)} %constant.109.clone.1, s32[]{:T(128)} %constant.110.clone.1) | dynamic-update-slice | bytes 12036 | tf_op jit(solution)/shard_map/scatter | solution.py:44
  182.5 3.3 %collective-permute-start.23 = (f32[4,8,1,128]{3,1,2,0:T(8,128)S(1)}, f32[4,8,1,128]{3,1,2,0:T(8,128)S(1)}, u32[]{:S(2)}, u32[]{:S(2)}) collective-permute-start(f32[4,8,1,128]{3,1,2,0:T(8,128)S(1)} %get-tuple-element.75), channel_id=1, source_target_pairs={{4,0},{8,4},{12,8},{0,12},{5,1},{9,5},{13,9},{1,13},{6,2},{10,6},{... | collective-permute-start | bytes 49160 | tf_op jit(solution)/shard_map/ppermute | solution.py:27
  185.8 1.9 collective-permute-done.22
  192.1 3.5 %collective-permute-start.27 = (f32[4,8,47]{2,1,0:T(8,128)S(1)}, f32[4,8,47]{2,1,0:T(8,128)S(1)}, u32[]{:S(2)}, u32[]{:S(2)}) collective-permute-start(f32[4,8,47]{2,1,0:T(8,128)S(1)} %collective-permute-done.26), channel_id=1, source_target_pairs={{0,8},{4,12},{8,0},{12,4},{1,9},{5,13},{9,1},{13,5},{2,10},{6,14},... | collective-permute-start | bytes 18056 | tf_op jit(solution)/shard_map/ppermute | solution.py:14
  198.2 2.2 pad_maximum_fusion.3
  201.8 16.0 %scatter.19 = f32[4,8,47,130]{3,1,2,0:T(8,128)S(1)} dynamic-update-slice(f32[4,8,47,130]{3,1,2,0:T(8,128)S(1)} %pad_maximum_fusion.3, f32[4,8,47,1]{3,1,2,0:T(8,128)} %copy.122, s32[]{:T(128)} %constant.109.clone.1, s32[]{:T(128)} %constant.109.clone.1, s32[]{:T(128)} %constant.109.clone.1, s32[]{:T(128)} %constant.110.clone.1) | dynamic-update-slice | bytes 12036 | tf_op jit(solution)/shard_map/scatter | solution.py:44
  (220 shorter events, 75.2 us)
Async XLA Ops:
  6.5 31.9 %all-gather.2.cloned.1.call-start = ((), (), s32[]{:S(2)}) async-start(), calls=%async_computation | async-start | bytes 1769472 | tf_op jit(solution)/shard_map/all_gather | solution.py:112
  39.7 5.6 %collective-permute-start = (f32[4,8,1,128]{3,1,2,0:T(8,128)S(1)}, f32[4,8,1,128]{3,1,2,0:T(8,128)S(1)}, u32[]{:S(2)}, u32[]{:S(2)}) collective-permute-start(f32[4,8,1,128]{3,1,2,0:T(8,128)S(1)} %get-tuple-element.80), channel_id=1, source_target_pairs={{0,4},{4,8},{8,12},{12,0},{1,5},{5,9},{9,13},{13,1},{2,6},{6,10},{... | collective-permute-start | bytes 49160 | tf_op jit(solution)/shard_map/ppermute | solution.py:24
  47.0 12.7 %collective-permute-start.3 = (f32[4,8,47,1]{2,1,0,3:T(8,128)S(1)}, f32[4,8,47,1]{2,1,0,3:T(8,128)S(1)}, u32[]{:S(2)}, u32[]{:S(2)}) collective-permute-start(f32[4,8,47,1]{2,1,0,3:T(8,128)S(1)} %copy.124), channel_id=1, source_target_pairs={{1,0},{3,2},{5,4},{7,6},{9,8},{11,10},{13,12},{15,14},{17,16},{19,... | collective-permute-start | bytes 18056 | tf_op jit(solution)/shard_map/ppermute | solution.py:27
  48.3 10.1 %collective-permute-start.2 = (f32[4,8,47,1]{2,1,0,3:T(8,128)}, f32[4,8,47,1]{2,1,0,3:T(8,128)S(1)}, u32[]{:S(2)}, u32[]{:S(2)}) collective-permute-start(f32[4,8,47,1]{2,1,0,3:T(8,128)} %copy.123), channel_id=1, source_target_pairs={{0,1},{2,3},{4,5},{6,7},{8,9},{10,11},{12,13},{14,15},{16,17},{18,... | collective-permute-start | bytes 18056 | tf_op jit(solution)/shard_map/ppermute | solution.py:24
  51.3 5.7 %collective-permute-start.4 = (f32[4,8,47]{2,1,0:T(8,128)}, f32[4,8,47]{2,1,0:T(8,128)}, u32[]{:S(2)}, u32[]{:S(2)}) collective-permute-start(f32[4,8,47]{2,1,0:T(8,128)} %bitcast.7), channel_id=1, source_target_pairs={{0,4},{4,0},{8,12},{12,8},{1,5},{5,1},{9,13},{13,9},{2,6},{6,2},{1... | collective-permute-start | bytes 18056 | tf_op jit(solution)/shard_map/ppermute | solution.py:14
  53.1 9.8 %collective-permute-start.6 = (f32[6,8,1,128]{3,2,0,1:T(1,128)}, f32[6,8,1,128]{3,2,0,1:T(1,128)S(1)}, u32[]{:S(2)}, u32[]{:S(2)}) collective-permute-start(f32[6,8,1,128]{3,2,0,1:T(1,128)} %get-tuple-element.64), channel_id=1, source_target_pairs={{0,4},{4,8},{8,12},{12,0},{1,5},{5,9},{9,13},{13,1},{2,6},{6,10},{... | collective-permute-start | bytes 73736 | tf_op jit(solution)/shard_map/ppermute | solution.py:24
  54.1 8.9 %collective-permute-start.7 = (f32[6,8,1,128]{3,2,0,1:T(1,128)}, f32[6,8,1,128]{3,2,0,1:T(1,128)S(1)}, u32[]{:S(2)}, u32[]{:S(2)}) collective-permute-start(f32[6,8,1,128]{3,2,0,1:T(1,128)} %get-tuple-element.65), channel_id=1, source_target_pairs={{4,0},{8,4},{12,8},{0,12},{5,1},{9,5},{13,9},{1,13},{6,2},{10,6},{... | collective-permute-start | bytes 73736 | tf_op jit(solution)/shard_map/ppermute | solution.py:27
  57.0 19.4 %collective-permute-start.5 = (f32[4,8,47]{2,1,0:T(8,128)}, f32[4,8,47]{2,1,0:T(8,128)}, u32[]{:S(2)}, u32[]{:S(2)}) collective-permute-start(f32[4,8,47]{2,1,0:T(8,128)} %collective-permute-done.4), channel_id=1, source_target_pairs={{0,8},{4,12},{8,0},{12,4},{1,9},{5,13},{9,1},{13,5},{2,10},{6,14},... | collective-permute-start | bytes 18056 | tf_op jit(solution)/shard_map/ppermute | solution.py:14
  70.8 27.0 %collective-permute-start.9 = (f32[6,8,47,1]{2,1,3,0:T(8,128)}, f32[6,8,47,1]{2,1,3,0:T(8,128)}, u32[]{:S(2)}, u32[]{:S(2)}) collective-permute-start(f32[6,8,47,1]{2,1,3,0:T(8,128)} %copy.105), channel_id=1, source_target_pairs={{1,0},{3,2},{5,4},{7,6},{9,8},{11,10},{13,12},{15,14},{17,16},{19,... | collective-permute-start | bytes 27080 | tf_op jit(solution)/shard_map/ppermute | solution.py:27
  72.1 23.4 %collective-permute-start.8 = (f32[6,8,47,1]{2,1,3,0:T(8,128)}, f32[6,8,47,1]{2,1,3,0:T(8,128)}, u32[]{:S(2)}, u32[]{:S(2)}) collective-permute-start(f32[6,8,47,1]{2,1,3,0:T(8,128)} %copy.99), channel_id=1, source_target_pairs={{0,1},{2,3},{4,5},{6,7},{8,9},{10,11},{12,13},{14,15},{16,17},{18,... | collective-permute-start | bytes 27080 | tf_op jit(solution)/shard_map/ppermute | solution.py:24
  105.4 5.6 %collective-permute-start.10 = (f32[4,8,1,128]{3,1,2,0:T(8,128)S(1)}, f32[4,8,1,128]{3,1,2,0:T(8,128)S(1)}, u32[]{:S(2)}, u32[]{:S(2)}) collective-permute-start(f32[4,8,1,128]{3,1,2,0:T(8,128)S(1)} %get-tuple-element.78), channel_id=1, source_target_pairs={{0,4},{4,8},{8,12},{12,0},{1,5},{5,9},{9,13},{13,1},{2,6},{6,10},{... | collective-permute-start | bytes 49160 | tf_op jit(solution)/shard_map/ppermute | solution.py:24
  112.0 7.1 %collective-permute-start.12 = (f32[4,8,47,1]{2,1,0,3:T(8,128)S(1)}, f32[4,8,47,1]{2,1,0,3:T(8,128)S(1)}, u32[]{:S(2)}, u32[]{:S(2)}) collective-permute-start(f32[4,8,47,1]{2,1,0,3:T(8,128)S(1)} %copy.125), channel_id=1, source_target_pairs={{0,1},{2,3},{4,5},{6,7},{8,9},{10,11},{12,13},{14,15},{16,17},{18,... | collective-permute-start | bytes 18056 | tf_op jit(solution)/shard_map/ppermute | solution.py:24
  113.6 5.9 %collective-permute-start.13 = (f32[4,8,47,1]{2,1,0,3:T(8,128)S(1)}, f32[4,8,47,1]{2,1,0,3:T(8,128)S(1)}, u32[]{:S(2)}, u32[]{:S(2)}) collective-permute-start(f32[4,8,47,1]{2,1,0,3:T(8,128)S(1)} %copy.126), channel_id=1, source_target_pairs={{1,0},{3,2},{5,4},{7,6},{9,8},{11,10},{13,12},{15,14},{17,16},{19,... | collective-permute-start | bytes 18056 | tf_op jit(solution)/shard_map/ppermute | solution.py:27
  115.4 7.1 %collective-permute-start.15 = (f32[4,8,47]{2,1,0:T(8,128)S(1)}, f32[4,8,47]{2,1,0:T(8,128)S(1)}, u32[]{:S(2)}, u32[]{:S(2)}) collective-permute-start(f32[4,8,47]{2,1,0:T(8,128)S(1)} %collective-permute-done.14), channel_id=1, source_target_pairs={{0,8},{4,12},{8,0},{12,4},{1,9},{5,13},{9,1},{13,5},{2,10},{6,14},... | collective-permute-start | bytes 18056 | tf_op jit(solution)/shard_map/ppermute | solution.py:14
  142.2 5.8 %collective-permute-start.16 = (f32[4,8,1,128]{3,1,2,0:T(8,128)S(1)}, f32[4,8,1,128]{3,1,2,0:T(8,128)S(1)}, u32[]{:S(2)}, u32[]{:S(2)}) collective-permute-start(f32[4,8,1,128]{3,1,2,0:T(8,128)S(1)} %get-tuple-element.76), channel_id=1, source_target_pairs={{0,4},{4,8},{8,12},{12,0},{1,5},{5,9},{9,13},{13,1},{2,6},{6,10},{... | collective-permute-start | bytes 49160 | tf_op jit(solution)/shard_map/ppermute | solution.py:24
  143.0 5.0 %collective-permute-start.17 = (f32[4,8,1,128]{3,1,2,0:T(8,128)S(1)}, f32[4,8,1,128]{3,1,2,0:T(8,128)S(1)}, u32[]{:S(2)}, u32[]{:S(2)}) collective-permute-start(f32[4,8,1,128]{3,1,2,0:T(8,128)S(1)} %get-tuple-element.77), channel_id=1, source_target_pairs={{4,0},{8,4},{12,8},{0,12},{5,1},{9,5},{13,9},{1,13},{6,2},{10,6},{... | collective-permute-start | bytes 49160 | tf_op jit(solution)/shard_map/ppermute | solution.py:27
  148.7 7.4 %collective-permute-start.18 = (f32[4,8,47,1]{2,1,0,3:T(8,128)S(1)}, f32[4,8,47,1]{2,1,0,3:T(8,128)S(1)}, u32[]{:S(2)}, u32[]{:S(2)}) collective-permute-start(f32[4,8,47,1]{2,1,0,3:T(8,128)S(1)} %copy.127), channel_id=1, source_target_pairs={{0,1},{2,3},{4,5},{6,7},{8,9},{10,11},{12,13},{14,15},{16,17},{18,... | collective-permute-start | bytes 18056 | tf_op jit(solution)/shard_map/ppermute | solution.py:24
  150.9 6.6 %collective-permute-start.19 = (f32[4,8,47,1]{2,1,0,3:T(8,128)S(1)}, f32[4,8,47,1]{2,1,0,3:T(8,128)S(1)}, u32[]{:S(2)}, u32[]{:S(2)}) collective-permute-start(f32[4,8,47,1]{2,1,0,3:T(8,128)S(1)} %copy.128), channel_id=1, source_target_pairs={{1,0},{3,2},{5,4},{7,6},{9,8},{11,10},{13,12},{15,14},{17,16},{19,... | collective-permute-start | bytes 18056 | tf_op jit(solution)/shard_map/ppermute | solution.py:27
  152.5 8.5 %collective-permute-start.21 = (f32[4,8,47]{2,1,0:T(8,128)S(1)}, f32[4,8,47]{2,1,0:T(8,128)S(1)}, u32[]{:S(2)}, u32[]{:S(2)}) collective-permute-start(f32[4,8,47]{2,1,0:T(8,128)S(1)} %collective-permute-done.20), channel_id=1, source_target_pairs={{0,8},{4,12},{8,0},{12,4},{1,9},{5,13},{9,1},{13,5},{2,10},{6,14},... | collective-permute-start | bytes 18056 | tf_op jit(solution)/shard_map/ppermute | solution.py:14
  181.9 5.8 %collective-permute-start.22 = (f32[4,8,1,128]{3,1,2,0:T(8,128)S(1)}, f32[4,8,1,128]{3,1,2,0:T(8,128)S(1)}, u32[]{:S(2)}, u32[]{:S(2)}) collective-permute-start(f32[4,8,1,128]{3,1,2,0:T(8,128)S(1)} %get-tuple-element.74), channel_id=1, source_target_pairs={{0,4},{4,8},{8,12},{12,0},{1,5},{5,9},{9,13},{13,1},{2,6},{6,10},{... | collective-permute-start | bytes 49160 | tf_op jit(solution)/shard_map/ppermute | solution.py:24
  182.5 5.2 %collective-permute-start.23 = (f32[4,8,1,128]{3,1,2,0:T(8,128)S(1)}, f32[4,8,1,128]{3,1,2,0:T(8,128)S(1)}, u32[]{:S(2)}, u32[]{:S(2)}) collective-permute-start(f32[4,8,1,128]{3,1,2,0:T(8,128)S(1)} %get-tuple-element.75), channel_id=1, source_target_pairs={{4,0},{8,4},{12,8},{0,12},{5,1},{9,5},{13,9},{1,13},{6,2},{10,6},{... | collective-permute-start | bytes 49160 | tf_op jit(solution)/shard_map/ppermute | solution.py:27
  188.4 7.2 %collective-permute-start.24 = (f32[4,8,47,1]{2,1,0,3:T(8,128)S(1)}, f32[4,8,47,1]{2,1,0,3:T(8,128)S(1)}, u32[]{:S(2)}, u32[]{:S(2)}) collective-permute-start(f32[4,8,47,1]{2,1,0,3:T(8,128)S(1)} %copy.129), channel_id=1, source_target_pairs={{0,1},{2,3},{4,5},{6,7},{8,9},{10,11},{12,13},{14,15},{16,17},{18,... | collective-permute-start | bytes 18056 | tf_op jit(solution)/shard_map/ppermute | solution.py:24
  190.5 6.4 %collective-permute-start.25 = (f32[4,8,47,1]{2,1,0,3:T(8,128)S(1)}, f32[4,8,47,1]{2,1,0,3:T(8,128)S(1)}, u32[]{:S(2)}, u32[]{:S(2)}) collective-permute-start(f32[4,8,47,1]{2,1,0,3:T(8,128)S(1)} %copy.130), channel_id=1, source_target_pairs={{1,0},{3,2},{5,4},{7,6},{9,8},{11,10},{13,12},{15,14},{17,16},{19,... | collective-permute-start | bytes 18056 | tf_op jit(solution)/shard_map/ppermute | solution.py:27
  192.1 8.3 %collective-permute-start.27 = (f32[4,8,47]{2,1,0:T(8,128)S(1)}, f32[4,8,47]{2,1,0:T(8,128)S(1)}, u32[]{:S(2)}, u32[]{:S(2)}) collective-permute-start(f32[4,8,47]{2,1,0:T(8,128)S(1)} %collective-permute-done.26), channel_id=1, source_target_pairs={{0,8},{4,12},{8,0},{12,4},{1,9},{5,13},{9,1},{13,5},{2,10},{6,14},... | collective-permute-start | bytes 18056 | tf_op jit(solution)/shard_map/ppermute | solution.py:14
  (49 other events, 213.7 us)
Sparse Core Ops, SparseCore 0:
  13.0 25.4 all-gather.1
where the time goes:
time: 230 us; the launch traced here: 228 us
  local copies, waits for them, and re-layouts  104 us (45%)
  starting transfers between devices  51.9 us (23%)
  waiting for transfers between devices  33.3 us (14%)
  other arithmetic  24.5 us (11%)
  between operations  14.3 us (6%)
    scatter x4, local copies, waits for them, and re-layouts, mirror_fold(): return framed.at[:, :, :, above].set(top_row)  62.2 us
    all_gather x1, waiting for transfers between devices, local(): whole_fields = lax.all_gather(stacked, 'trc', axis=1, tiled=True)  25.6 us
    ppermute x10, starting transfers between devices, padded_2(): lax.ppermute(lax.slice_in_dim(block, 0, width, axis=dim), axis, backward)  20.8 us
    ppermute x10, starting transfers between devices, padded_2(): lax.ppermute(lax.slice_in_dim(block, block.shape[dim] - width, None, axis...  17.3 us
    ppermute x8, starting transfers between devices, from_partner(): lax.ppermute(array, axis, [(i, i ^ 1 << bit) for i in range(lax.axis_size...  13.9 us
    unnamed x101, local copies, waits for them, and re-layouts  12.8 us
    concatenate x9, other arithmetic, padded_2(): block = jnp.concatenate([low, block, high], axis=dim)  8.63 us
    ppermute x5, local copies, waits for them, and re-layouts, padded_2(): lax.ppermute(lax.slice_in_dim(block, 0, width, axis=dim), axis, backward)  7.35 us
  transfers between devices with their start and end apart: 29, of which 8 were waited for; matrix products, arithmetic and copies ran while one was open for 21% of the time, Pallas kernels for 0%

commit v1 on v0

v1 whole, which is shorter than its diff:
```python
import functools

import jax
import jax.numpy as jnp
from jax import lax
from jax.experimental import pallas as pl
from jax.experimental.pallas import tpu as pltpu
from jax.sharding import PartitionSpec as P

SUBSTEPS = 4
time_step = 0.8
pulse_height = 1.0
MESH = pl.DeviceIdType.MESH
OFF = 8


def tile_starts(columns):
    half = -(-columns // 16)
    return [8 * a for a in range(half)] + [columns - 8 - 8 * a for a in reversed(range(half))]


def kernel(
    n_trc, n_gx, tr, col, mask, u_in, v_in, m_in, se_in, sn_in, out,
    ph, mk, west_edge, east_edge, side, west_land, east_land, side_land,
    coef, fx, row_send, lane_send, row_land, lane_land, halo,
    own_sem, gs_sem, gr_sem, es_sem, er_sem, hs_sem, hr_sem,
):
    tracers, levels, columns, lanes = tr.shape
    own = mask.shape[0]
    starts = tile_starts(columns)
    tiles = len(starts)
    me, gx, gy = lax.axis_index("trc"), lax.axis_index("gx"), lax.axis_index("gy")
    east = lax.rem(gx + 1, n_gx)
    west = lax.rem(gx + n_gx - 1, n_gx)
    other, mirror = 1 - gy, n_gx - 1 - gx
    top = gy == 1
    lane = lax.broadcasted_iota(jnp.int32, (8, lanes), 1)
    row = lax.broadcasted_iota(jnp.int32, (8, lanes), 0)
    top_f = jnp.full((8, lanes), gy, jnp.int32).astype(jnp.float32)
    is_top = jnp.full((8, lanes), gy, jnp.int32) == 1

    barrier = pltpu.get_barrier_semaphore()
    for d in range(n_trc):
        p = lax.rem(me + d, n_trc)
        if d:
            pl.semaphore_signal(barrier, inc=1, device_id={"trc": p}, device_id_type=MESH)
        for where in ({"trc": p, "gx": east}, {"trc": p, "gx": west}, {"trc": p, "gy": other}):
            pl.semaphore_signal(barrier, inc=1, device_id=where, device_id_type=MESH)
    pl.semaphore_signal(barrier, inc=1, device_id={"gx": mirror}, device_id_type=MESH)
    pl.semaphore_wait(barrier, 4 * n_trc)

    mine = pl.ds(me * own, own)
    blocks = [(mask, mk.at[mine])] + [
        (ref, ph.at[f, mine]) for f, ref in enumerate((u_in, v_in, m_in, se_in, sn_in))
    ]
    gathers, locals_ = [], []
    for f, (src, dst) in enumerate(blocks):
        for d in range(1, n_trc):
            copy = pltpu.make_async_remote_copy(
                src_ref=src, dst_ref=dst, send_sem=gs_sem.at[f, d], recv_sem=gr_sem.at[f, d],
                device_id={"trc": lax.rem(me + d, n_trc)}, device_id_type=MESH,
            )
            copy.start()
            gathers.append(copy)
        copy = pltpu.make_async_copy(src, dst, own_sem.at[f])
        copy.start()
        locals_.append(copy)

    west_edge[...] = jnp.zeros_like(west_edge)
    east_edge[...] = jnp.zeros_like(east_edge)
    for l in range(own):
        for f, ref in enumerate((u_in, m_in, se_in)):
            west_edge[f, l : l + 1, :] = ref[l, columns - 1 : columns, :]
        west_edge[3, l : l + 1, :] = mask[l, columns - 1 : columns, :].astype(jnp.float32)
        east_edge[l : l + 1, :] = mask[l, 0:1, :].astype(jnp.float32)
    for r, start in enumerate(starts):
        acc = jnp.zeros((8, lanes), jnp.float32)
        for f, ref in enumerate((v_in, m_in, sn_in, mask)):
            for l in range(own):
                x = f * own + l
                value = ref[l, start : start + 8, :].astype(jnp.float32)
                acc = jnp.where(lane // 2 == x, pltpu.roll(value, 2 * x + 1, 1), acc)
        side[r] = acc
    edges = []
    for d in range(n_trc):
        p = lax.rem(me + d, n_trc)
        for e, (src, dst, where) in enumerate((
            (west_edge, west_land.at[me], {"trc": p, "gx": east}),
            (east_edge, east_land.at[me], {"trc": p, "gx": west}),
            (side, side_land.at[me], {"trc": p, "gy": other}),
        )):
            copy = pltpu.make_async_remote_copy(
                src_ref=src, dst_ref=dst, send_sem=es_sem.at[e, d], recv_sem=er_sem.at[e, d],
                device_id=where, device_id_type=MESH,
            )
            copy.start()
            edges.append(copy)

    def halo_copies(slot, t):
        def remote(src, dst, e, where):
            return pltpu.make_async_remote_copy(
                src_ref=src, dst_ref=dst, send_sem=hs_sem.at[e, t], recv_sem=hr_sem.at[e, slot, t],
                device_id=where, device_id_type=MESH,
            )

        return (
            remote(row_send.at[0, t], row_land.at[0, slot, t], 0, {"gx": west}),
            remote(row_send.at[1, t], row_land.at[1, slot, t], 1, {"gx": east}),
            remote(lane_send.at[t], lane_land.at[0, slot, t], 2, {"gy": other}),
            remote(lane_send.at[t], lane_land.at[1, slot, t], 3, {"gx": mirror}),
        )

    def pack(acc, value, k):
        return jnp.where(lane // 2 == k, pltpu.roll(value, 2 * k + 1, 1), acc)

    def start_halo(slot, t):
        for copy in halo_copies(slot, t):
            copy.start()

    for f in range(1):
        for copy in gathers[: n_trc - 1]:
            copy.wait_recv()
        locals_[0].wait()
    first_label = me * tracers

    def begin(t, carry):
        label = first_label + t
        for r, start in enumerate(starts):
            acc = jnp.zeros((8, lanes), jnp.float32)
            for k in range(levels):
                wet = mk[k, start : start + 8, :].astype(jnp.float32)
                hit = col[k, start : start + 8, :] == label
                value = tr[t, k, start : start + 8, :] + pulse_height * jnp.where(hit, wet, 0.0)
                fx[0, t, k, OFF + start : OFF + start + 8, :] = value
                acc = pack(acc, value, k)
                if r == 0:
                    row_send[0, t, k : k + 1, :] = value[0:1, :]
                if r == tiles - 1:
                    row_send[1, t, k : k + 1, :] = value[7:8, :]
            lane_send[t, r] = acc
        start_halo(0, t)
        return carry

    lax.fori_loop(0, tracers, begin, 0)

    for copy in gathers[n_trc - 1 :]:
        copy.wait_recv()
    for copy in locals_[1:]:
        copy.wait()
    for copy in edges:
        copy.wait_recv()

    def coefficients(p, carry):
        for l in range(own):
            k = p * own + l
            for r, start in enumerate(starts):
                here = slice(start, start + 8)

                def westward(load, f):
                    if start:
                        return load(slice(start - 1, start + 7))
                    edge = west_land[p, f, l : l + 1, :]
                    return jnp.where(row == 0, edge, pltpu.roll(load(here), 1, 0))

                def field(f):
                    return lambda rows: ph[f, k, rows, :]

                def wetness(rows):
                    return mk[k, rows, :].astype(jnp.float32)

                wet = wetness(here)
                if r < tiles - 1:
                    wet_e = wetness(slice(start + 1, start + 9))
                else:
                    wet_e = jnp.where(row == 7, east_land[p, l : l + 1, :], pltpu.roll(wet, 7, 0))
                sides = side_land[p, r]

                def southward(value, f):
                    edge = pltpu.roll(sides, (lanes - 2 * (f * own + l)) % lanes, 1)
                    return jnp.where(lane == 0, edge, pltpu.roll(value, 1, 1))

                wet_n = jnp.where(
                    lane == lanes - 1,
                    jnp.where(is_top, 1.0, pltpu.roll(sides, lanes - 2 - 2 * (3 * own + l), 1)),
                    pltpu.roll(wet, lanes - 1, 1),
                )
                wet_s = southward(wet, 3)
                wet_s = jnp.where((lane == 0) & jnp.logical_not(is_top), 0.0, wet_s)
                speed, mix, slope = field(0)(here), field(2)(here), field(3)(here)

                def parts(speed, mix, slope, opened):
                    opened = time_step * opened
                    return (
                        (jnp.maximum(speed, 0.0) + mix) * opened,
                        (mix - jnp.minimum(speed, 0.0)) * opened,
                        (0.25 * mix * slope) * opened,
                    )

                ae, be, ce = parts(speed, mix, slope, wet * wet_e)
                aw, bw, cw = parts(
                    westward(field(0), 0), westward(field(2), 1), westward(field(3), 2),
                    wet * westward(wetness, 3),
                )
                speed, slope = field(1)(here), field(4)(here)
                an, bn, cn = parts(speed, mix, slope, wet * wet_n)
                a_s, bs, cs = parts(
                    southward(speed, 0), southward(mix, 1), southward(slope, 2), wet * wet_s
                )
                values = (
                    1.0 - ((ae + bw) + (an + bs)), be, aw, bn, a_s,
                    (ce - cw) + (cn - cs), ce, cw, cn, cs,
                )
                for c, value in enumerate(values):
                    coef[c, k, r] = value
        return carry

    lax.fori_loop(0, n_trc, coefficients, 0)

    def step(it, carry):
        s, t = it // tracers, lax.rem(it, tracers)
        now = lax.rem(s, 2)
        later = 1 - now
        for copy in halo_copies(now, t):
            copy.wait()
        from_east, from_west = row_land[0, now, t], row_land[1, now, t]
        for k in range(levels):
            fx[now, t, k, OFF - 1 : OFF, :] = from_west[k : k + 1, :]
            fx[now, t, k, OFF + columns : OFF + columns + 1, :] = from_east[k : k + 1, :]
        for r, start in enumerate(starts):
            near = lane_land[0, now, t, r]
            far = lane_land[1, now, t, tiles - 1 - r]
            for bit in (1, 2, 4):
                far = jnp.where((row & bit) == 0, pltpu.roll(far, 8 - bit, 0), pltpu.roll(far, bit, 0))
            upper = jnp.where((lane & 1) == 0, far, pltpu.roll(near, 1, 1))
            border = jnp.where(is_top, upper, pltpu.roll(near, lanes - 1, 1))
            at = OFF + start
            here, e, w, n, s_ = [], [], [], [], []
            for k in range(levels):
                f = fx[now, t, k, at : at + 8, :]
                here.append(f)
                e.append(fx[now, t, k, at + 1 : at + 9, :])
                w.append(fx[now, t, k, at - 1 : at + 7, :])
                ends = pltpu.roll(border, lanes - 1 - 2 * k, 1)
                n.append(jnp.where(lane == lanes - 1, ends, pltpu.roll(f, lanes - 1, 1)))
                s_.append(jnp.where(lane == 0, ends, pltpu.roll(f, 1, 1)))

            def dz(a, k):
                if k == 0:
                    return a[1]
                if k == levels - 1:
                    return -a[k - 1]
                return a[k + 1] - a[k - 1]

            acc = jnp.zeros((8, lanes), jnp.float32)
            for k in range(levels):
                c = [coef[i, k, r] for i in range(10)]
                value = (
                    (c[0] * here[k] + c[5] * dz(here, k))
                    + (c[1] * e[k] + c[6] * dz(e, k))
                    + (c[2] * w[k] - c[7] * dz(w, k))
                    + (c[3] * n[k] + c[8] * dz(n, k))
                    + (c[4] * s_[k] - c[9] * dz(s_, k))
                )
                fx[later, t, k, at : at + 8, :] = value
                acc = pack(acc, value, k)
                if r == 0:
                    row_send[0, t, k : k + 1, :] = value[0:1, :]
                if r == tiles - 1:
                    row_send[1, t, k : k + 1, :] = value[7:8, :]
            lane_send[t, r] = acc

        @pl.when(s < SUBSTEPS - 1)
        def _():
            start_halo(later, t)

        return carry

    lax.fori_loop(0, SUBSTEPS * tracers, step, 0)

    last = SUBSTEPS % 2

    def finish(t, carry):
        for k in range(levels):
            for start in starts:
                out[t, k, start : start + 8, :] = fx[last, t, k, OFF + start : OFF + start + 8, :]
        return carry

    lax.fori_loop(0, tracers, finish, 0)
    for copy in gathers + edges:
        copy.wait_send()


def local(n_trc, n_gx, *args):
    tracers, levels, columns, lanes = args[0].shape
    tiles = len(tile_starts(columns))
    f32 = jnp.float32
    vmem = pl.BlockSpec(memory_space=pltpu.VMEM)
    rows = -(-(OFF + columns + 1) // 8) * 8
    dma = pltpu.SemaphoreType.DMA
    return pl.pallas_call(
        functools.partial(kernel, n_trc, n_gx),
        out_shape=jax.ShapeDtypeStruct(args[0].shape, f32),
        in_specs=[vmem] * 8,
        out_specs=vmem,
        scratch_shapes=[
            pltpu.VMEM((5, levels, columns, lanes), f32),
            pltpu.VMEM((levels, columns, lanes), jnp.int32),
            pltpu.VMEM((4, 8, lanes), f32),
            pltpu.VMEM((8, lanes), f32),
            pltpu.VMEM((tiles, 8, lanes), f32),
            pltpu.VMEM((n_trc, 4, 8, lanes), f32),
            pltpu.VMEM((n_trc, 8, lanes), f32),
            pltpu.VMEM((n_trc, tiles, 8, lanes), f32),
            pltpu.VMEM((10, levels, tiles, 8, lanes), f32),
            pltpu.VMEM((2, tracers, levels, rows, lanes), f32),
            pltpu.VMEM((2, tracers, 8, lanes), f32),
            pltpu.VMEM((tracers, tiles, 8, lanes), f32),
            pltpu.VMEM((2, 2, tracers, 8, lanes), f32),
            pltpu.VMEM((2, 2, tracers, tiles, 8, lanes), f32),
            pltpu.VMEM((tiles, 8, lanes), f32),
            dma((6,)), dma((6, n_trc)), dma((6, n_trc)), dma((3, n_trc)), dma((3, n_trc)),
            dma((4, tracers)), dma((4, 2, tracers)),
        ],
        compiler_params=pltpu.CompilerParams(
            collective_id=0, has_side_effects=True, vmem_limit_bytes=40 * 1024 * 1024
        ),
    )(*args)


def solution(mesh):
    field = P("trc", "gx", "gy")
    in_specs = (P(("grp", "trc"), None, "gx", "gy"), P(None, "gx", "gy")) + (field,) * 6
    return jax.shard_map(
        functools.partial(local, mesh.shape["trc"], mesh.shape["gx"]),
        mesh=mesh, in_specs=in_specs, out_specs=in_specs[0], check_vma=False,
    )
```

time: 230 us -> 44.5 us (0.19)
  local copies, waits for them, and re-layouts: 104 us -> 5.06 us
  starting transfers between devices: 51.9 us -> 0 us
  Pallas kernels: 0 us -> 39.2 us
  waiting for transfers between devices: 33.3 us -> 0 us
  other arithmetic: 24.5 us -> 0 us
  between operations: 14.3 us -> 0.08 us
    scatter x4 -> x0, local copies, waits for them, and re-layouts: 62.2 us -> none  [mirror_fold(): return framed.at[:, :, :, above].set(top_row)]
    ppermute x28 -> x0, starting transfers between devices: 51.9 us -> none  [the longest x10 20.8 us: padded_2(): lax.ppermute(lax.slice_in_dim(block, 0, width, axis=dim), axis, backward)]
    pallas_call x0 -> x1, Pallas kernels: none -> 39.2 us  [local(): pl.pallas_call(functools.partial(kernel, n_trc, n_gx), out_shape=jax.Shap...]
    all_gather x1 -> x0, waiting for transfers between devices: 25.6 us -> none  [local(): whole_fields = lax.all_gather(stacked, 'trc', axis=1, tiled=True)]
    ppermute x10 -> x0, local copies, waits for them, and re-layouts: 13.9 us -> none  [the longest x5 7.35 us: padded_2(): lax.ppermute(lax.slice_in_dim(block, 0, width, axis=dim), axis, backward)]
    mul x17 -> x0, other arithmetic: 11.5 us -> none  [the longest x5 5.28 us: advance_window(): (jnp.maximum(north_speed, 0.0) * here_y + jnp.minimum(north_speed, 0.0) *...]
    unnamed x101 -> x16, local copies, waits for them, and re-layouts: 12.8 us -> 3.97 us
    concatenate x9 -> x0, other arithmetic: 8.63 us -> none  [padded_2(): block = jnp.concatenate([low, block, high], axis=dim)]
  transfers between devices with their start and end apart: 29 -> 0, of which waited for: 8 -> 0; matrix products, arithmetic and copies ran while one was open for 21% -> 0% of each run, Pallas kernels for 0% -> 0%
where the time goes in v1:
time: 44.5 us; the launch traced here: 44.3 us
  Pallas kernels  39.2 us (88%)
  local copies, waits for them, and re-layouts  5.06 us (11%)
    pallas_call x1, Pallas kernels, local(): pl.pallas_call(functools.partial(kernel, n_trc, n_gx), out_shape=jax.Shap...  39.2 us
    unnamed x16, local copies, waits for them, and re-layouts  3.97 us
    pallas_call x1, local copies, waits for them, and re-layouts, local(): pl.pallas_call(functools.partial(kernel, n_trc, n_gx), out_shape=jax.Shap...  1.09 us

profile of v1, /device:TPU:0, one launch (start us, length us, event | category | flops | bytes accessed | tf_op | source)
XLA Modules:
  0.0 44.3 jit_solution(1109851178405509540)
XLA Ops:
  0.0 0.0 copy-start.2
  0.0 0.0 copy-start
  0.0 1.0 %copy.11.mask = s32[4,45,128]{2,1,0:T(8,128)S(1)} copy(s32[4,45,128]{2,0,1:T(4,128)} %param.10) | data formatting | bytes 184320 | tf_op args[2]
  1.0 0.0 copy-done.2
  1.0 0.9 %copy.13.v_in = f32[4,45,128]{2,1,0:T(8,128)S(1)} copy(f32[4,45,128]{2,0,1:T(4,128)} %param.12) | data formatting | bytes 184320 | tf_op args[4]
  1.9 0.0 copy-start.3
  1.9 0.9 %copy.14.m_in = f32[4,45,128]{2,1,0:T(8,128)S(1)} copy(f32[4,45,128]{2,0,1:T(4,128)} %param.13) | data formatting | bytes 184320 | tf_op args[5]
  2.8 0.0 copy-start.1
  2.9 0.9 %copy.15.se_in = f32[4,45,128]{2,1,0:T(8,128)S(1)} copy(f32[4,45,128]{2,0,1:T(4,128)} %param.14) | data formatting | bytes 184320 | tf_op args[6]
  3.8 0.0 copy-done.3
  3.8 0.0 copy-done.1
  3.9 0.0 copy-done
  3.9 0.1 copy.9.tr
  4.0 39.2 %shard_map.82 = f32[4,8,45,128]{3,2,1,0:T(8,128)S(1)} custom-call(f32[4,8,45,128]{3,2,1,0:T(8,128)S(1)} %copy.9.tr, s32[8,45,128]{2,1,0:T(8,128)S(1)} %copy.10.col, s32[4,45,128]{2,1,0:T(8,128)S(1)} %copy.11.mask, f32[4,45,128]{2,1,0:T(8,128)S(1)} %copy.12.u_in, f32[4,45,128]{2,1,0:T(8,128)S(1)} %copy.13.v_in, f32[4,45,128]{2,1,0:T(8,128)S(1)} %copy.14.m_in, ...), custom_call_target="tpu_custom_call" | custom-call | tf_op jit(solution)/shard_map/pallas_call | solution.py:300
  43.2 1.1 %copy.17 = f32[4,8,45,128]{3,1,2,0:T(8,128)} copy(f32[4,8,45,128]{3,2,1,0:T(8,128)S(1)} %shard_map.82) | data formatting | bytes 1474560 | tf_op jit(solution)/shard_map/pallas_call | solution.py:300
  (3 shorter events, 0.1 us)
Async XLA Ops:
  0.0 1.0 %copy-start.2 = (f32[4,45,128]{2,0,1:T(4,128)S(1)}, f32[4,45,128]{2,0,1:T(4,128)}, u32[]{:S(2)}) copy-start(f32[4,45,128]{2,0,1:T(4,128)} %param.11) | copy-start | bytes 276484
  0.0 3.9 %copy-start = (f32[4,8,45,128]{3,1,2,0:T(8,128)S(1)}, f32[4,8,45,128]{3,1,2,0:T(8,128)}, u32[]{:S(2)}) copy-start(f32[4,8,45,128]{3,1,2,0:T(8,128)} %param.8) | copy-start | bytes 2211844
  1.9 1.9 %copy-start.3 = (f32[4,45,128]{2,0,1:T(4,128)S(1)}, f32[4,45,128]{2,0,1:T(4,128)}, u32[]{:S(2)}) copy-start(f32[4,45,128]{2,0,1:T(4,128)} %param.15) | copy-start | bytes 276484
  2.8 1.0 %copy-start.1 = (s32[8,45,128]{2,0,1:T(8,128)S(1)}, s32[8,45,128]{2,0,1:T(8,128)}, u32[]{:S(2)}) copy-start(s32[8,45,128]{2,0,1:T(8,128)} %param.9) | copy-start | bytes 552964

commit v2 on v0

v2 whole, which is shorter than its diff:
```python
import functools

import jax
import jax.numpy as jnp
from jax import lax
from jax.experimental import pallas as pl
from jax.experimental.pallas import tpu as pltpu
from jax.sharding import PartitionSpec as P

SUBSTEPS = 4
time_step = 0.8
pulse_height = 1.0
MESH = pl.DeviceIdType.MESH


def kernel(
    n_trc, n_gx, group, tr, col, mask, u_in, v_in, m_in, se_in, sn_in, out,
    ph, big, west_edge, east_edge, side, west_land, east_land, side_land, shore,
    coef, rim, fx, lane_send, lane_land,
    gs_sem, gr_sem, fs_sem, fr_sem, es_sem, er_sem, hs_sem, hr_sem,
):
    tracers, columns, levels, lanes = tr.shape
    own = mask.shape[1]
    me, gx, gy, grp = (lax.axis_index(a) for a in ("trc", "gx", "gy", "grp"))
    east = lax.rem(gx + 1, n_gx)
    west = lax.rem(gx + n_gx - 1, n_gx)
    other, mirror, twin = 1 - gy, n_gx - 1 - gx, 1 - grp
    tile = (levels, lanes)
    lane = lax.broadcasted_iota(jnp.int32, tile, 1)
    row = lax.broadcasted_iota(jnp.int32, tile, 0)
    pair_of = lane // 2
    is_top = jnp.full(tile, gy, jnp.int32) == 1
    last = lanes - 1

    barrier = pltpu.get_barrier_semaphore()
    for d in range(n_trc):
        p = lax.rem(me + d, n_trc)
        if d:
            pl.semaphore_signal(barrier, inc=1, device_id={"trc": p}, device_id_type=MESH)
        for where in ({"trc": p, "gx": east}, {"trc": p, "gx": west}, {"trc": p, "gy": other}):
            pl.semaphore_signal(barrier, inc=1, device_id=where, device_id_type=MESH)
    pl.semaphore_signal(barrier, inc=1, device_id={"gx": mirror}, device_id_type=MESH)
    pl.semaphore_signal(barrier, inc=1, device_id={"grp": twin}, device_id_type=MESH)

    sources = (mask, m_in, u_in, v_in, se_in, sn_in)
    for f, ref in enumerate(sources):
        def stage(i, carry, f=f, ref=ref):
            ph[f, me, i] = ref[i].astype(jnp.float32)
            return carry

        lax.fori_loop(0, columns, stage, 0, unroll=True)
    for e, ref in enumerate((mask, m_in, u_in, se_in)):
        west_edge[e] = ref[columns - 1].astype(jnp.float32)
    east_edge[...] = mask[0].astype(jnp.float32)

    pl.semaphore_wait(barrier, 4 * n_trc + 1)

    def remote(src, dst, send, recv, where):
        return pltpu.make_async_remote_copy(
            src_ref=src, dst_ref=dst, send_sem=send, recv_sem=recv,
            device_id=where, device_id_type=MESH,
        )

    def gather(q, d):
        block = ph.at[2 * q + grp, me]
        return remote(
            block, block, gs_sem.at[q, d], gr_sem.at[q, d], {"trc": lax.rem(me + d, n_trc)}
        )

    def forward(q, d):
        block = ph.at[2 * q + grp, lax.rem(me + n_trc - d, n_trc)]
        return remote(block, block, fs_sem.at[q, d], fr_sem.at[q, d], {"grp": twin})

    others = range(1, n_trc)
    for q in range(3):
        for d in others:
            gather(q, d).start()

    half = lax.broadcasted_iota(jnp.int32, (own, lanes), 1) // 2
    for e, ref in enumerate((mask, m_in, v_in, sn_in)):
        acc = jnp.zeros((own, lanes), jnp.float32)
        for i in range(columns):
            value = ref[i].astype(jnp.float32)
            acc = jnp.where(half == i, pltpu.roll(value, 2 * i + 1, 1), acc)
        side[e] = acc
    edges = []
    for d in range(n_trc):
        p = lax.rem(me + d, n_trc)
        for e, (src, dst, where) in enumerate((
            (west_edge, west_land.at[me], {"trc": p, "gx": east}),
            (east_edge, east_land.at[me], {"trc": p, "gx": west}),
            (side, side_land.at[me], {"trc": p, "gy": other}),
        )):
            copy = remote(src, dst, es_sem.at[e, d], er_sem.at[e, d], where)
            copy.start()
            edges.append(copy)

    def halo_copies(slot, t):
        ts = pl.ds(t, group)

        def send(src, dst, e, where):
            return remote(src, dst, hs_sem.at[e, t], hr_sem.at[e, slot, t], where)

        return (
            send(fx.at[slot, ts, 1], fx.at[slot, ts, columns + 1], 0, {"gx": west}),
            send(fx.at[slot, ts, columns], fx.at[slot, ts, 0], 1, {"gx": east}),
            send(lane_send.at[0, ts], lane_land.at[0, slot, ts], 2, {"gy": other}),
            send(lane_send.at[1, ts], lane_land.at[1, slot, ts], 3, {"gx": mirror}),
        )

    def start_halo(slot, t):
        copies = halo_copies(slot, t)
        for copy in copies[:3]:
            copy.start()

        @pl.when(gy == 1)
        def _():
            copies[3].start()

    def wait_halo(slot, t):
        copies = halo_copies(slot, t)
        for copy in copies[:3]:
            copy.wait()

        @pl.when(gy == 1)
        def _():
            copies[3].wait()

    def pack(packs, value, i):
        near, far = packs
        near = jnp.where(pair_of == i, pltpu.roll(value, 2 * i + 1, 1), near)
        back = 2 * (columns - 1 - i)
        far = jnp.where(lane == back, pltpu.roll(value, back + 1, 1), far)
        return near, far

    def pass_on(q):
        for d in others:
            gather(q, d).wait_recv()
            forward(q, d).start()

    def assemble(f):
        for p in range(n_trc):
            def put(i, carry, p=p):
                big[f, i + 1, p * own : (p + 1) * own, :] = ph[f, p, i]
                return carry

            lax.fori_loop(0, columns, put, 0, unroll=True)

    pass_on(0)
    for d in others:
        forward(0, d).wait_recv()
    assemble(0)
    assemble(1)
    first_label = me * tracers
    zero = jnp.zeros(tile, jnp.float32)

    def begin(t):
        packs = [(zero, zero)] * group
        for i in range(columns):
            for a in range(group):
                hit = col[i] == first_label + (t + a)
                value = tr[t + a, i] + pulse_height * jnp.where(hit, big[0, i + 1], 0.0)
                fx[0, t + a, i + 1] = value
                packs[a] = pack(packs[a], value, i)
        for a in range(group):
            lane_send[0, t + a], lane_send[1, t + a] = packs[a]
        start_halo(0, t)

    batches = tracers // group
    for b in range(batches):
        begin(b * group)
        if b == 0:
            pass_on(1)
    pass_on(2)
    for copy in edges:
        copy.wait_recv()
    for e, f in enumerate((0, 1, 2, 4)):
        for p in range(n_trc):
            big[f, 0, p * own : (p + 1) * own, :] = west_land[p, e]
    for p in range(n_trc):
        big[0, columns + 1, p * own : (p + 1) * own, :] = east_land[p]
        for e in range(4):
            shore[e, p * own : (p + 1) * own, :] = side_land[p, e]
    for q in (1, 2):
        for d in others:
            forward(q, d).wait_recv()
        assemble(2 * q)
        assemble(2 * q + 1)

    def parts(speed, mix, slope, opened):
        opened = time_step * opened
        return (
            (jnp.maximum(speed, 0.0) + mix) * opened,
            (mix - jnp.minimum(speed, 0.0)) * opened,
            (0.25 * mix * slope) * opened,
        )

    def east_face(at):
        return parts(big[2, at], big[1, at], big[4, at], big[0, at] * big[0, at + 1])

    aw, bw, cw = east_face(0)
    rim_f, rim_z = zero, zero
    for i in range(columns):
        at = i + 1
        ae, be, ce = east_face(at)
        wet, mix, speed, slope = big[0, at], big[1, at], big[3, at], big[5, at]

        def southward(value, e):
            edge = pltpu.roll(shore[e], (lanes - 2 * i) % lanes, 1)
            return jnp.where(lane == 0, edge, pltpu.roll(value, 1, 1))

        above = jnp.where(is_top, 1.0, pltpu.roll(shore[0], (lanes - 2 - 2 * i) % lanes, 1))
        wet_n = jnp.where(lane == last, above, pltpu.roll(wet, last, 1))
        wet_s = jnp.where((lane > 0) | is_top, southward(wet, 0), 0.0)
        an, bn, cn = parts(speed, mix, slope, wet * wet_n)
        a_s, bs, cs = parts(
            southward(speed, 2), southward(mix, 1), southward(slope, 3), wet * wet_s
        )
        values = (
            1.0 - ((ae + bw) + (an + bs)), (ce - cw) + (cn - cs), be, ce, aw, cw,
            jnp.where(lane == last, 0.0, an), jnp.where(lane == last, 0.0, cn),
            jnp.where(lane == 0, 0.0, bs), jnp.where(lane == 0, 0.0, cs),
        )
        for c, value in enumerate(values):
            coef[c, i] = value
        here = pair_of == i
        rim_f = jnp.where(here, pltpu.roll(jnp.where(lane == last, bn, a_s), 2 * i + 1, 1), rim_f)
        rim_z = jnp.where(here, pltpu.roll(jnp.where(lane == last, cn, -cs), 2 * i + 1, 1), rim_z)
        aw, bw, cw = ae, be, ce
    rim[0], rim[1] = rim_f, rim_z

    def dz(f):
        upper = jnp.where(row < levels - 1, pltpu.roll(f, levels - 1, 0), 0.0)
        return upper - jnp.where(row > 0, pltpu.roll(f, 1, 0), 0.0)

    edge_lane = (lane == 0) | (lane == last)

    def step(it, carry):
        s, t = it // batches, lax.rem(it, batches) * group
        now = lax.rem(s, 2)
        later = 1 - now
        wait_halo(now, t)
        border, packs, window = [], [], []
        for a in range(group):
            near, far = lane_land[0, now, t + a], lane_land[1, now, t + a]
            upper = jnp.where((lane & 1) == 0, far, pltpu.roll(near, 1, 1))
            ends = jnp.where(is_top, upper, pltpu.roll(near, last, 1))
            border.append(rim[0] * ends + rim[1] * dz(ends))
            packs.append((zero, zero))
            f0, f1 = fx[now, t + a, 0], fx[now, t + a, 1]
            window.append((f0, dz(f0), f1, dz(f1)))
        for i in range(columns):
            c = [coef[x, i] for x in range(10)]
            for a in range(group):
                fw, zw, f, z = window[a]
                fe = fx[now, t + a, i + 2]
                ze = dz(fe)
                window[a] = (f, z, fe, ze)
                ends = pltpu.roll(border[a], (lanes - 1 - 2 * i) % lanes, 1)
                value = (
                    (c[0] * f + c[1] * z)
                    + (c[2] * fe + c[3] * ze)
                    + (c[4] * fw - c[5] * zw)
                    + (pltpu.roll(c[6] * f - c[7] * z, 1, 1) + pltpu.roll(c[8] * f + c[9] * z, last, 1))
                    + jnp.where(edge_lane, ends, 0.0)
                )
                fx[later, t + a, i + 1] = value
                packs[a] = pack(packs[a], value, i)
        for a in range(group):
            lane_send[0, t + a], lane_send[1, t + a] = packs[a]

        @pl.when(s < SUBSTEPS - 1)
        def _():
            start_halo(later, t)

        return carry

    lax.fori_loop(0, SUBSTEPS * batches, step, 0)

    final = SUBSTEPS % 2
    for t in range(tracers):
        for i in range(columns):
            out[t, i] = fx[final, t, i + 1]
    for copy in edges:
        copy.wait_send()
    for q in range(3):
        for d in others:
            gather(q, d).wait_send()
            forward(q, d).wait_send()


def local(n_trc, n_gx, tracers, colors, *fields):
    f32 = jnp.float32
    held = jnp.transpose(tracers, (0, 2, 1, 3))
    count, columns, levels, lanes = held.shape
    own = fields[0].shape[0]
    moved = [jnp.transpose(a, (1, 0, 2)) for a in (colors,) + fields]
    vmem = pl.BlockSpec(memory_space=pltpu.VMEM)
    dma = pltpu.SemaphoreType.DMA
    group = 2 if count % 2 == 0 else 1
    result = pl.pallas_call(
        functools.partial(kernel, n_trc, n_gx, group),
        out_shape=jax.ShapeDtypeStruct(held.shape, f32),
        in_specs=[vmem] * 8,
        out_specs=vmem,
        scratch_shapes=[
            pltpu.VMEM((6, n_trc, columns, own, lanes), f32),
            pltpu.VMEM((6, columns + 2, levels, lanes), f32),
            pltpu.VMEM((4, own, lanes), f32),
            pltpu.VMEM((own, lanes), f32),
            pltpu.VMEM((4, own, lanes), f32),
            pltpu.VMEM((n_trc, 4, own, lanes), f32),
            pltpu.VMEM((n_trc, own, lanes), f32),
            pltpu.VMEM((n_trc, 4, own, lanes), f32),
            pltpu.VMEM((4, levels, lanes), f32),
            pltpu.VMEM((10, columns, levels, lanes), f32),
            pltpu.VMEM((2, levels, lanes), f32),
            pltpu.VMEM((2, count, columns + 2, levels, lanes), f32),
            pltpu.VMEM((2, count, levels, lanes), f32),
            pltpu.VMEM((2, 2, count, levels, lanes), f32),
            dma((3, n_trc)), dma((3, n_trc)), dma((3, n_trc)), dma((3, n_trc)),
            dma((3, n_trc)), dma((3, n_trc)), dma((4, count)), dma((4, 2, count)),
        ],
        compiler_params=pltpu.CompilerParams(
            collective_id=0, has_side_effects=True, vmem_limit_bytes=40 * 1024 * 1024
        ),
    )(held, *moved)
    return jnp.transpose(result, (0, 2, 1, 3))


def solution(mesh):
    field = P("trc", "gx", "gy")
    in_specs = (P(("grp", "trc"), None, "gx", "gy"), P(None, "gx", "gy")) + (field,) * 6
    return jax.shard_map(
        functools.partial(local, mesh.shape["trc"], mesh.shape["gx"]),
        mesh=mesh, in_specs=in_specs, out_specs=in_specs[0], check_vma=False,
    )
```

time: 230 us -> 63.5 us (0.28)
  local copies, waits for them, and re-layouts: 104 us -> 8.24 us
  Pallas kernels: 0 us -> 54.8 us
  starting transfers between devices: 51.9 us -> 0 us
  waiting for transfers between devices: 33.3 us -> 0 us
  other arithmetic: 24.5 us -> 0 us
  between operations: 14.3 us -> 0.02 us
    scatter x4 -> x0, local copies, waits for them, and re-layouts: 62.2 us -> none  [mirror_fold(): return framed.at[:, :, :, above].set(top_row)]
    pallas_call x0 -> x1, Pallas kernels: none -> 54.8 us  [local(): pl.pallas_call(functools.partial(kernel, n_trc, n_gx, group), out_shape=j...]
    ppermute x28 -> x0, starting transfers between devices: 51.9 us -> none  [the longest x10 20.8 us: padded_2(): lax.ppermute(lax.slice_in_dim(block, 0, width, axis=dim), axis, backward)]
    all_gather x1 -> x0, waiting for transfers between devices: 25.6 us -> none  [local(): whole_fields = lax.all_gather(stacked, 'trc', axis=1, tiled=True)]
    ppermute x10 -> x0, local copies, waits for them, and re-layouts: 13.9 us -> none  [the longest x5 7.35 us: padded_2(): lax.ppermute(lax.slice_in_dim(block, 0, width, axis=dim), axis, backward)]
    mul x17 -> x0, other arithmetic: 11.5 us -> none  [the longest x5 5.28 us: advance_window(): (jnp.maximum(north_speed, 0.0) * here_y + jnp.minimum(north_speed, 0.0) *...]
    concatenate x9 -> x0, other arithmetic: 8.63 us -> none  [padded_2(): block = jnp.concatenate([low, block, high], axis=dim)]
    ppermute x28 -> x0, waiting for transfers between devices: 7.69 us -> none  [the longest x10 6.75 us: padded_2(): lax.ppermute(lax.slice_in_dim(block, block.shape[dim] - width, None, axis...]
  transfers between devices with their start and end apart: 29 -> 0, of which waited for: 8 -> 0; matrix products, arithmetic and copies ran while one was open for 21% -> 0% of each run, Pallas kernels for 0% -> 0%
where the time goes in v2:
time: 63.5 us; the launch traced here: 63.1 us
  Pallas kernels  54.8 us (86%)
  local copies, waits for them, and re-layouts  8.24 us (13%)
    pallas_call x1, Pallas kernels, local(): pl.pallas_call(functools.partial(kernel, n_trc, n_gx, group), out_shape=j...  54.8 us
    unnamed x17, local copies, waits for them, and re-layouts  8.24 us

profile of v2, /device:TPU:0, one launch (start us, length us, event | category | flops | bytes accessed | tf_op | source)
XLA Modules:
  0.0 63.1 jit_solution(3177337566613918847)
XLA Ops:
  0.0 0.0 copy-start
  0.0 1.1 %copy-done = f32[4,8,45,128]{3,1,2,0:T(8,128)S(1)} copy-done((f32[4,8,45,128]{3,1,2,0:T(8,128)S(1)}, f32[4,8,45,128]{3,1,2,0:T(8,128)}, u32[]{:S(2)}) %copy-start) | copy-done | bytes 737304
  1.1 0.0 copy-start.1
  1.1 0.9 %copy-done.1 = s32[8,45,128]{2,0,1:T(8,128)S(1)} copy-done((s32[8,45,128]{2,0,1:T(8,128)S(1)}, s32[8,45,128]{2,0,1:T(8,128)}, u32[]{:S(2)}) %copy-start.1) | copy-done | bytes 184344
  2.0 0.0 copy-start.2
  2.0 0.9 %copy-done.2 = s32[4,45,128]{2,0,1:T(4,128)S(1)} copy-done((s32[4,45,128]{2,0,1:T(4,128)S(1)}, s32[4,45,128]{2,0,1:T(4,128)}, u32[]{:S(2)}) %copy-start.2) | copy-done | bytes 92184
  2.9 0.0 copy-start.3
  2.9 0.9 %copy-done.3 = f32[4,45,128]{2,0,1:T(4,128)S(1)} copy-done((f32[4,45,128]{2,0,1:T(4,128)S(1)}, f32[4,45,128]{2,0,1:T(4,128)}, u32[]{:S(2)}) %copy-start.3) | copy-done | bytes 92184
  3.8 0.0 copy-start.4
  3.8 0.9 %copy-done.4 = f32[4,45,128]{2,0,1:T(4,128)S(1)} copy-done((f32[4,45,128]{2,0,1:T(4,128)S(1)}, f32[4,45,128]{2,0,1:T(4,128)}, u32[]{:S(2)}) %copy-start.4) | copy-done | bytes 92184
  4.7 0.0 copy-start.5
  4.7 0.9 %copy-done.5 = f32[4,45,128]{2,0,1:T(4,128)S(1)} copy-done((f32[4,45,128]{2,0,1:T(4,128)S(1)}, f32[4,45,128]{2,0,1:T(4,128)}, u32[]{:S(2)}) %copy-start.5) | copy-done | bytes 92184
  5.6 0.0 copy-start.6
  5.6 0.9 %copy-done.6 = f32[4,45,128]{2,0,1:T(4,128)S(1)} copy-done((f32[4,45,128]{2,0,1:T(4,128)S(1)}, f32[4,45,128]{2,0,1:T(4,128)}, u32[]{:S(2)}) %copy-start.6) | copy-done | bytes 92184
  6.5 0.0 copy-start.7
  6.5 0.9 %copy-done.7 = f32[4,45,128]{2,0,1:T(4,128)S(1)} copy-done((f32[4,45,128]{2,0,1:T(4,128)S(1)}, f32[4,45,128]{2,0,1:T(4,128)}, u32[]{:S(2)}) %copy-start.7) | copy-done | bytes 92184
  7.4 54.8 %shard_map.82 = f32[4,45,8,128]{3,2,1,0:T(8,128)S(1)} custom-call(f32[4,45,8,128]{3,2,1,0:T(8,128)S(1)} %bitcast.10, s32[45,8,128]{2,1,0:T(8,128)S(1)} %bitcast.11, s32[45,4,128]{2,1,0:T(4,128)S(1)} %bitcast.12, f32[45,4,128]{2,1,0:T(4,128)S(1)} %bitcast.13, f32[45,4,128]{2,1,0:T(4,128)S(1)} %bitcast.14, f32[45,4,128]{2,1,0:T(4,128)S(1)} %bitcast.15, ...), custom_call_target="tpu_custom_call" | custom-call | tf_op jit(solution)/shard_map/pallas_call | solution.py:301
  62.2 0.9 %copy.10 = f32[4,8,45,128]{3,1,2,0:T(8,128)} copy(f32[4,8,45,128]{3,1,2,0:T(8,128)S(1)} %bitcast.9) | data formatting | bytes 1474560
Async XLA Ops:
  0.0 1.1 %copy-start = (f32[4,8,45,128]{3,1,2,0:T(8,128)S(1)}, f32[4,8,45,128]{3,1,2,0:T(8,128)}, u32[]{:S(2)}) copy-start(f32[4,8,45,128]{3,1,2,0:T(8,128)} %param.8) | copy-start | bytes 2211844
  1.1 0.9 %copy-start.1 = (s32[8,45,128]{2,0,1:T(8,128)S(1)}, s32[8,45,128]{2,0,1:T(8,128)}, u32[]{:S(2)}) copy-start(s32[8,45,128]{2,0,1:T(8,128)} %param.9) | copy-start | bytes 552964
  2.0 0.9 %copy-start.2 = (s32[4,45,128]{2,0,1:T(4,128)S(1)}, s32[4,45,128]{2,0,1:T(4,128)}, u32[]{:S(2)}) copy-start(s32[4,45,128]{2,0,1:T(4,128)} %param.10) | copy-start | bytes 276484
  2.9 0.9 %copy-start.3 = (f32[4,45,128]{2,0,1:T(4,128)S(1)}, f32[4,45,128]{2,0,1:T(4,128)}, u32[]{:S(2)}) copy-start(f32[4,45,128]{2,0,1:T(4,128)} %param.11) | copy-start | bytes 276484
  3.8 0.9 %copy-start.4 = (f32[4,45,128]{2,0,1:T(4,128)S(1)}, f32[4,45,128]{2,0,1:T(4,128)}, u32[]{:S(2)}) copy-start(f32[4,45,128]{2,0,1:T(4,128)} %param.12) | copy-start | bytes 276484
  4.7 0.9 %copy-start.5 = (f32[4,45,128]{2,0,1:T(4,128)S(1)}, f32[4,45,128]{2,0,1:T(4,128)}, u32[]{:S(2)}) copy-start(f32[4,45,128]{2,0,1:T(4,128)} %param.13) | copy-start | bytes 276484
  5.6 0.9 %copy-start.6 = (f32[4,45,128]{2,0,1:T(4,128)S(1)}, f32[4,45,128]{2,0,1:T(4,128)}, u32[]{:S(2)}) copy-start(f32[4,45,128]{2,0,1:T(4,128)} %param.14) | copy-start | bytes 276484
  6.5 0.9 %copy-start.7 = (f32[4,45,128]{2,0,1:T(4,128)S(1)}, f32[4,45,128]{2,0,1:T(4,128)}, u32[]{:S(2)}) copy-start(f32[4,45,128]{2,0,1:T(4,128)} %param.15) | copy-start | bytes 276484

commit v3 on v2

--- a/solution.py
+++ b/solution.py
@@ -14,9 +14,11 @@
 
 
 def kernel(
-    n_trc, n_gx, group, tr, col, mask, u_in, v_in, m_in, se_in, sn_in, out,
+    n_trc, n_gx, group,
+    tr_h, col_h, mask_h, u_h, v_h, m_h, se_h, sn_h, out,
+    tr, col, mask, u_in, v_in, m_in, se_in, sn_in, in_sem,
     ph, big, west_edge, east_edge, side, west_land, east_land, side_land, shore,
-    coef, rim, fx, lane_send, lane_land,
+    coef, rim, faces, bent, fx, lane_send, lane_land,
     gs_sem, gr_sem, fs_sem, fr_sem, es_sem, er_sem, hs_sem, hr_sem,
 ):
     tracers, columns, levels, lanes = tr.shape
@@ -28,9 +30,18 @@
     tile = (levels, lanes)
     lane = lax.broadcasted_iota(jnp.int32, tile, 1)
     row = lax.broadcasted_iota(jnp.int32, tile, 0)
-    pair_of = lane // 2
     is_top = jnp.full(tile, gy, jnp.int32) == 1
     last = lanes - 1
+
+    loads = [
+        pltpu.make_async_copy(src, dst, in_sem.at[n])
+        for n, (src, dst) in enumerate((
+            (mask_h, mask), (m_h, m_in), (u_h, u_in), (v_h, v_in), (se_h, se_in), (sn_h, sn_in),
+            (col_h, col), (tr_h, tr),
+        ))
+    ]
+    for copy in loads:
+        copy.start()
 
     barrier = pltpu.get_barrier_semaphore()
     for d in range(n_trc):
@@ -41,6 +52,9 @@
             pl.semaphore_signal(barrier, inc=1, device_id=where, device_id_type=MESH)
     pl.semaphore_signal(barrier, inc=1, device_id={"gx": mirror}, device_id_type=MESH)
     pl.semaphore_signal(barrier, inc=1, device_id={"grp": twin}, device_id_type=MESH)
+
+    for copy in loads[:6]:
+        copy.wait()
 
     sources = (mask, m_in, u_in, v_in, se_in, sn_in)
     for f, ref in enumerate(sources):
@@ -95,6 +109,27 @@
             copy.start()
             edges.append(copy)
 
+    def tile_at(c, shift=0):
+        return pl.ds(levels * (c + 1) + shift, levels)
+
+    flat = faces.shape[1]
+    ends_of = (((row == 0) & (lane == last)) | ((row == 1) & (lane == 0))).astype(jnp.float32)
+
+    def edge_rows(value):
+        return lax.dot_general(
+            ends_of, value, (((1,), (1,)), ((), ())),
+            precision=lax.Precision.HIGHEST, preferred_element_type=jnp.float32,
+        )
+
+    def pack(slot, t):
+        body = [fx[slot, t, 2 * levels : (2 + columns) * levels, :]]
+        if flat > columns * levels:
+            body.append(fx[slot, t, 2 * levels : 2 * levels + flat - columns * levels, :])
+        lane_send[0, t] = edge_rows(jnp.concatenate(body, axis=0))
+        turned = [fx[slot, t, tile_at(columns - i), :] for i in range(columns)]
+        turned += turned[:1] * (flat // levels - columns)
+        lane_send[1, t] = edge_rows(jnp.concatenate(turned, axis=0))
+
     def halo_copies(slot, t):
         ts = pl.ds(t, group)
 
@@ -102,8 +137,8 @@
             return remote(src, dst, hs_sem.at[e, t], hr_sem.at[e, slot, t], where)
 
         return (
-            send(fx.at[slot, ts, 1], fx.at[slot, ts, columns + 1], 0, {"gx": west}),
-            send(fx.at[slot, ts, columns], fx.at[slot, ts, 0], 1, {"gx": east}),
+            send(fx.at[slot, ts, tile_at(1)], fx.at[slot, ts, tile_at(columns + 1)], 0, {"gx": west}),
+            send(fx.at[slot, ts, tile_at(columns)], fx.at[slot, ts, tile_at(0)], 1, {"gx": east}),
             send(lane_send.at[0, ts], lane_land.at[0, slot, ts], 2, {"gy": other}),
             send(lane_send.at[1, ts], lane_land.at[1, slot, ts], 3, {"gx": mirror}),
         )
@@ -125,13 +160,6 @@
         @pl.when(gy == 1)
         def _():
             copies[3].wait()
-
-    def pack(packs, value, i):
-        near, far = packs
-        near = jnp.where(pair_of == i, pltpu.roll(value, 2 * i + 1, 1), near)
-        back = 2 * (columns - 1 - i)
-        far = jnp.where(lane == back, pltpu.roll(value, back + 1, 1), far)
-        return near, far
 
     def pass_on(q):
         for d in others:
@@ -146,24 +174,23 @@
 
             lax.fori_loop(0, columns, put, 0, unroll=True)
 
+    for copy in loads[6:]:
+        copy.wait()
     pass_on(0)
     for d in others:
         forward(0, d).wait_recv()
     assemble(0)
     assemble(1)
     first_label = me * tracers
-    zero = jnp.zeros(tile, jnp.float32)
 
     def begin(t):
-        packs = [(zero, zero)] * group
         for i in range(columns):
             for a in range(group):
                 hit = col[i] == first_label + (t + a)
                 value = tr[t + a, i] + pulse_height * jnp.where(hit, big[0, i + 1], 0.0)
-                fx[0, t + a, i + 1] = value
-                packs[a] = pack(packs[a], value, i)
+                fx[0, t + a, tile_at(i + 1), :] = value
         for a in range(group):
-            lane_send[0, t + a], lane_send[1, t + a] = packs[a]
+            pack(0, t + a)
         start_halo(0, t)
 
     batches = tracers // group
@@ -199,7 +226,6 @@
         return parts(big[2, at], big[1, at], big[4, at], big[0, at] * big[0, at + 1])
 
     aw, bw, cw = east_face(0)
-    rim_f, rim_z = zero, zero
     for i in range(columns):
         at = i + 1
         ae, be, ce = east_face(at)
@@ -223,54 +249,64 @@
         )
         for c, value in enumerate(values):
             coef[c, i] = value
-        here = pair_of == i
-        rim_f = jnp.where(here, pltpu.roll(jnp.where(lane == last, bn, a_s), 2 * i + 1, 1), rim_f)
-        rim_z = jnp.where(here, pltpu.roll(jnp.where(lane == last, cn, -cs), 2 * i + 1, 1), rim_z)
+        faces[0, levels * i : levels * (i + 1), :] = jnp.where(lane == last, bn, a_s)
+        faces[1, levels * i : levels * (i + 1), :] = jnp.where(lane == last, cn, -cs)
         aw, bw, cw = ae, be, ce
-    rim[0], rim[1] = rim_f, rim_z
-
-    def dz(f):
-        upper = jnp.where(row < levels - 1, pltpu.roll(f, levels - 1, 0), 0.0)
-        return upper - jnp.where(row > 0, pltpu.roll(f, 1, 0), 0.0)
-
-    edge_lane = (lane == 0) | (lane == last)
+    for c in range(2):
+        rim[c] = edge_rows(faces[c])
+
+    flat_lane = lax.broadcasted_iota(jnp.int32, (8, flat), 1)
+    flat_row = lax.broadcasted_iota(jnp.int32, (8, flat), 0)
+    flat_level = lax.rem(flat_lane, levels)
+    flat_top = jnp.full((8, flat), gy, jnp.int32) == 1
+
+    def flat_dz(f):
+        upper = jnp.where(flat_level < levels - 1, pltpu.roll(f, flat - 1, 1), 0.0)
+        return upper - jnp.where(flat_level > 0, pltpu.roll(f, 1, 1), 0.0)
 
     def step(it, carry):
         s, t = it // batches, lax.rem(it, batches) * group
         now = lax.rem(s, 2)
         later = 1 - now
         wait_halo(now, t)
-        border, packs, window = [], [], []
+
+        def dz(a, c):
+            upper = jnp.where(row < levels - 1, fx[now, t + a, tile_at(c, 1), :], 0.0)
+            return upper - jnp.where(row > 0, fx[now, t + a, tile_at(c, -1), :], 0.0)
+
+        window = []
         for a in range(group):
             near, far = lane_land[0, now, t + a], lane_land[1, now, t + a]
-            upper = jnp.where((lane & 1) == 0, far, pltpu.roll(near, 1, 1))
-            ends = jnp.where(is_top, upper, pltpu.roll(near, last, 1))
-            border.append(rim[0] * ends + rim[1] * dz(ends))
-            packs.append((zero, zero))
-            f0, f1 = fx[now, t + a, 0], fx[now, t + a, 1]
-            window.append((f0, dz(f0), f1, dz(f1)))
+            upper = jnp.where(flat_row == 0, far, pltpu.roll(near, 1, 0))
+            ends = jnp.where(flat_top, upper, pltpu.roll(near, 7, 0))
+            ends = jnp.where(flat_row < 2, rim[0] * ends + rim[1] * flat_dz(ends), 0.0)
+            bent[a] = lax.dot_general(
+                ends, ends_of, (((0,), (0,)), ((), ())),
+                precision=lax.Precision.HIGHEST, preferred_element_type=jnp.float32,
+            )
+            window.append((
+                fx[now, t + a, tile_at(0), :], dz(a, 0), fx[now, t + a, tile_at(1), :], dz(a, 1)
+            ))
         for i in range(columns):
             c = [coef[x, i] for x in range(10)]
             for a in range(group):
                 fw, zw, f, z = window[a]
-                fe = fx[now, t + a, i + 2]
-                ze = dz(fe)
+                fe = fx[now, t + a, tile_at(i + 2), :]
+                ze = dz(a, i + 2)
                 window[a] = (f, z, fe, ze)
-                ends = pltpu.roll(border[a], (lanes - 1 - 2 * i) % lanes, 1)
                 value = (
                     (c[0] * f + c[1] * z)
                     + (c[2] * fe + c[3] * ze)
                     + (c[4] * fw - c[5] * zw)
                     + (pltpu.roll(c[6] * f - c[7] * z, 1, 1) + pltpu.roll(c[8] * f + c[9] * z, last, 1))
-                    + jnp.where(edge_lane, ends, 0.0)
+                    + bent[a, levels * i : levels * (i + 1), :]
                 )
-                fx[later, t + a, i + 1] = value
-                packs[a] = pack(packs[a], value, i)
-        for a in range(group):
-            lane_send[0, t + a], lane_send[1, t + a] = packs[a]
+                fx[later, t + a, tile_at(i + 1), :] = value
 
         @pl.when(s < SUBSTEPS - 1)
         def _():
+            for a in range(group):
+                pack(later, t + a)
             start_halo(later, t)
 
         return carry
@@ -280,7 +316,7 @@
     final = SUBSTEPS % 2
     for t in range(tracers):
         for i in range(columns):
-            out[t, i] = fx[final, t, i + 1]
+            out[t, i] = fx[final, t, tile_at(i + 1), :]
     for copy in edges:
         copy.wait_send()
     for q in range(3):
@@ -297,13 +333,15 @@
     moved = [jnp.transpose(a, (1, 0, 2)) for a in (colors,) + fields]
     vmem = pl.BlockSpec(memory_space=pltpu.VMEM)
     dma = pltpu.SemaphoreType.DMA
+    flat = -(-columns * levels // 128) * 128
     group = 2 if count % 2 == 0 else 1
     result = pl.pallas_call(
         functools.partial(kernel, n_trc, n_gx, group),
         out_shape=jax.ShapeDtypeStruct(held.shape, f32),
-        in_specs=[vmem] * 8,
+        in_specs=[pl.BlockSpec(memory_space=pltpu.HBM)] * 8,
         out_specs=vmem,
-        scratch_shapes=[
+        scratch_shapes=[pltpu.VMEM(a.shape, a.dtype) for a in [held] + moved] + [
+            dma((8,)),
             pltpu.VMEM((6, n_trc, columns, own, lanes), f32),
             pltpu.VMEM((6, columns + 2, levels, lanes), f32),
             pltpu.VMEM((4, own, lanes), f32),
@@ -314,10 +352,12 @@
             pltpu.VMEM((n_trc, 4, own, lanes), f32),
             pltpu.VMEM((4, levels, lanes), f32),
             pltpu.VMEM((10, columns, levels, lanes), f32),
-            pltpu.VMEM((2, levels, lanes), f32),
-            pltpu.VMEM((2, count, columns + 2, levels, lanes), f32),
-            pltpu.VMEM((2, count, levels, lanes), f32),
-            pltpu.VMEM((2, 2, count, levels, lanes), f32),
+            pltpu.VMEM((2, 8, flat), f32),
+            pltpu.VMEM((2, flat, lanes), f32),
+            pltpu.VMEM((group, flat, lanes), f32),
+            pltpu.VMEM((2, count, flat + 4 * levels, lanes), f32),
+            pltpu.VMEM((2, count, 8, flat), f32),
+            pltpu.VMEM((2, 2, count, 8, flat), f32),
             dma((3, n_trc)), dma((3, n_trc)), dma((3, n_trc)), dma((3, n_trc)),
             dma((3, n_trc)), dma((3, n_trc)), dma((4, count)), dma((4, 2, count)),
         ],

time: 63.5 us -> 49.1 us (0.77)
  Pallas kernels: 54.8 us -> 40.4 us
    pallas_call x1, Pallas kernels: 54.8 us -> 40.4 us  [local(): pl.pallas_call(functools.partial(kernel, n_trc, n_gx, group), out_shape=j...]
where the time goes in v3:
time: 49.1 us; the launch traced here: 48.7 us
  Pallas kernels  40.4 us (82%)
  local copies, waits for them, and re-layouts  8.24 us (17%)
    pallas_call x1, Pallas kernels, local(): pl.pallas_call(functools.partial(kernel, n_trc, n_gx, group), out_shape=j...  40.4 us
    unnamed x17, local copies, waits for them, and re-layouts  8.24 us

profile of v3, /device:TPU:0, one launch (start us, length us, event | category | flops | bytes accessed | tf_op | source)
XLA Modules:
  0.0 48.7 jit_solution(17836565579491013619)
XLA Ops:
  0.0 0.0 copy-start
  0.0 1.1 %copy-done = f32[4,8,45,128]{3,1,2,0:T(8,128)S(1)} copy-done((f32[4,8,45,128]{3,1,2,0:T(8,128)S(1)}, f32[4,8,45,128]{3,1,2,0:T(8,128)}, u32[]{:S(2)}) %copy-start) | copy-done | bytes 737304
  1.1 0.0 copy-start.1
  1.1 0.9 %copy-done.1 = s32[8,45,128]{2,0,1:T(8,128)S(1)} copy-done((s32[8,45,128]{2,0,1:T(8,128)S(1)}, s32[8,45,128]{2,0,1:T(8,128)}, u32[]{:S(2)}) %copy-start.1) | copy-done | bytes 184344
  2.0 0.0 copy-start.2
  2.0 0.9 %copy-done.2 = s32[4,45,128]{2,0,1:T(4,128)S(1)} copy-done((s32[4,45,128]{2,0,1:T(4,128)S(1)}, s32[4,45,128]{2,0,1:T(4,128)}, u32[]{:S(2)}) %copy-start.2) | copy-done | bytes 92184
  2.9 0.0 copy-start.3
  2.9 0.9 %copy-done.3 = f32[4,45,128]{2,0,1:T(4,128)S(1)} copy-done((f32[4,45,128]{2,0,1:T(4,128)S(1)}, f32[4,45,128]{2,0,1:T(4,128)}, u32[]{:S(2)}) %copy-start.3) | copy-done | bytes 92184
  3.8 0.0 copy-start.4
  3.8 0.9 %copy-done.4 = f32[4,45,128]{2,0,1:T(4,128)S(1)} copy-done((f32[4,45,128]{2,0,1:T(4,128)S(1)}, f32[4,45,128]{2,0,1:T(4,128)}, u32[]{:S(2)}) %copy-start.4) | copy-done | bytes 92184
  4.7 0.0 copy-start.5
  4.7 0.9 %copy-done.5 = f32[4,45,128]{2,0,1:T(4,128)S(1)} copy-done((f32[4,45,128]{2,0,1:T(4,128)S(1)}, f32[4,45,128]{2,0,1:T(4,128)}, u32[]{:S(2)}) %copy-start.5) | copy-done | bytes 92184
  5.6 0.0 copy-start.6
  5.6 0.9 %copy-done.6 = f32[4,45,128]{2,0,1:T(4,128)S(1)} copy-done((f32[4,45,128]{2,0,1:T(4,128)S(1)}, f32[4,45,128]{2,0,1:T(4,128)}, u32[]{:S(2)}) %copy-start.6) | copy-done | bytes 92184
  6.5 0.0 copy-start.7
  6.5 0.9 %copy-done.7 = f32[4,45,128]{2,0,1:T(4,128)S(1)} copy-done((f32[4,45,128]{2,0,1:T(4,128)S(1)}, f32[4,45,128]{2,0,1:T(4,128)}, u32[]{:S(2)}) %copy-start.7) | copy-done | bytes 92184
  7.4 40.4 %shard_map.82 = f32[4,45,8,128]{3,2,1,0:T(8,128)S(1)} custom-call(f32[4,45,8,128]{3,2,1,0:T(8,128)S(1)} %bitcast.10, s32[45,8,128]{2,1,0:T(8,128)S(1)} %bitcast.11, s32[45,4,128]{2,1,0:T(4,128)S(1)} %bitcast.12, f32[45,4,128]{2,1,0:T(4,128)S(1)} %bitcast.13, f32[45,4,128]{2,1,0:T(4,128)S(1)} %bitcast.14, f32[45,4,128]{2,1,0:T(4,128)S(1)} %bitcast.15, ...), custom_call_target="tpu_custom_call" | custom-call | tf_op jit(solution)/shard_map/pallas_call | solution.py:338
  47.8 0.9 %copy.10 = f32[4,8,45,128]{3,1,2,0:T(8,128)} copy(f32[4,8,45,128]{3,1,2,0:T(8,128)S(1)} %bitcast.9) | data formatting | bytes 1474560
Async XLA Ops:
  0.0 1.1 %copy-start = (f32[4,8,45,128]{3,1,2,0:T(8,128)S(1)}, f32[4,8,45,128]{3,1,2,0:T(8,128)}, u32[]{:S(2)}) copy-start(f32[4,8,45,128]{3,1,2,0:T(8,128)} %param.8) | copy-start | bytes 2211844
  1.1 0.9 %copy-start.1 = (s32[8,45,128]{2,0,1:T(8,128)S(1)}, s32[8,45,128]{2,0,1:T(8,128)}, u32[]{:S(2)}) copy-start(s32[8,45,128]{2,0,1:T(8,128)} %param.9) | copy-start | bytes 552964
  2.0 0.9 %copy-start.2 = (s32[4,45,128]{2,0,1:T(4,128)S(1)}, s32[4,45,128]{2,0,1:T(4,128)}, u32[]{:S(2)}) copy-start(s32[4,45,128]{2,0,1:T(4,128)} %param.10) | copy-start | bytes 276484
  2.9 0.9 %copy-start.3 = (f32[4,45,128]{2,0,1:T(4,128)S(1)}, f32[4,45,128]{2,0,1:T(4,128)}, u32[]{:S(2)}) copy-start(f32[4,45,128]{2,0,1:T(4,128)} %param.11) | copy-start | bytes 276484
  3.8 0.9 %copy-start.4 = (f32[4,45,128]{2,0,1:T(4,128)S(1)}, f32[4,45,128]{2,0,1:T(4,128)}, u32[]{:S(2)}) copy-start(f32[4,45,128]{2,0,1:T(4,128)} %param.12) | copy-start | bytes 276484
  4.7 0.9 %copy-start.5 = (f32[4,45,128]{2,0,1:T(4,128)S(1)}, f32[4,45,128]{2,0,1:T(4,128)}, u32[]{:S(2)}) copy-start(f32[4,45,128]{2,0,1:T(4,128)} %param.13) | copy-start | bytes 276484
  5.6 0.9 %copy-start.6 = (f32[4,45,128]{2,0,1:T(4,128)S(1)}, f32[4,45,128]{2,0,1:T(4,128)}, u32[]{:S(2)}) copy-start(f32[4,45,128]{2,0,1:T(4,128)} %param.14) | copy-start | bytes 276484
  6.5 0.9 %copy-start.7 = (f32[4,45,128]{2,0,1:T(4,128)S(1)}, f32[4,45,128]{2,0,1:T(4,128)}, u32[]{:S(2)}) copy-start(f32[4,45,128]{2,0,1:T(4,128)} %param.15) | copy-start | bytes 276484
